TPU v7x, 512 devices: a whole 4x4x16 slice. The times are simulated.
512 devices in a mesh: pos: 32 (over z, core), trk: 16 (over y, x).
Axes of the slice: x: 4, y: 4, z: 16, core: 2. Of those that a mesh axis runs over, the one named last changes fastest.
Arguments:
- activations: bfloat16 [4, 16384, 1536], P(None, 'pos', 'trk'), may hold values from -6 to 6
- norm_gain: float32 [1536], P('trk'), may hold values from 0.1 to 1.9
- norm_bias: float32 [1536], P('trk'), may hold values from -1 to 1
- conv_weight: bfloat16 [3, 1536, 1536], P(None, None, 'trk'), may hold values from -0.09375 to 0.09375
- head_weight: bfloat16 [1536, 4096], P(None, 'trk'), may hold values from -0.15625 to 0.15625
- head_bias: float32 [4096], P('trk'), may hold values from -2 to 0
- gene_slot: int32 [4, 16384], P(None, 'pos'), may hold values from -1 to 35, as said below
- straddle_map: int32 [128], P('pos'), may hold values from -1 to 31, as said below
Outputs:
- tracks: bfloat16 [4, 16384, 4096], P(None, 'pos', 'trk')
- gene_mean: float32 [1024, 4096], P('pos', 'trk')
Inputs may be any that keep to these rules, and one draw needn't show every extreme that they name: `gene_slot`: -1 marks a bin outside exons. A value g below 32 names gene g of the bin's own block of 512 positions; 32 + s names entry s of the previous block's straddle list and appears only where that entry is not -1, never in the first block. `straddle_map`: entry index * 4 + s names the gene of block index that entry s of its straddle list stands for, or -1; the live entries of one block are distinct, and the last block's are all -1.
All inputs are finite; a program needn't handle non-finite values.
Results may differ from a plain program's by a relative error of at most 0.0048.
Values may be sent and summed in bfloat16 or wider, within the bound.
A program may use at most 128 MiB of HBM per device.

v0:
```python
import jax
import jax.numpy as jnp
from jax import lax
from jax.sharding import PartitionSpec as P

GENES_DEV = 32


def with_halo(cells, sides, width):
    for axis, dim in sides:
        count = lax.axis_size(axis)
        ends = count - 1
        head = lax.slice_in_dim(cells, 0, width, axis=dim)
        tail = lax.slice_in_dim(cells, cells.shape[dim] - width, cells.shape[dim], axis=dim)
        cells = jnp.concatenate(
            [
                lax.ppermute(tail, axis, [(i, (i + 1) % count) for i in range(ends)]),
                cells,
                lax.ppermute(head, axis, [((i + 1) % count, i) for i in range(ends)]),
            ],
            axis=dim,
        )
    return cells


def passed_along(value, axis, steps):
    count = lax.axis_size(axis)
    initial, last = (max(0, -steps), min(count, count - steps))
    return lax.ppermute(value, axis, [(source, source + steps) for source in range(initial, last)])


def per_device(
    activations, norm_gain, norm_bias, conv_weight, head_weight, head_bias, gene_slot, straddle_map
):
    sequences, length, channels = activations.shape
    total_rows = sequences * length
    hidden = jax.nn.gelu(
        activations.astype(jnp.float32) * norm_gain + norm_bias, approximate=True
    ).astype(jnp.bfloat16)
    zeros_init = jnp.zeros((total_rows, conv_weight.shape[2]), jnp.float32)
    gathered = lax.all_gather(hidden, "trk", axis=2, tiled=True)
    padded = with_halo(gathered, (("pos", 1),), 1)
    running = zeros_init
    columns = padded.shape[2]
    for tap_index in range(3):
        tap_rows = conv_weight[tap_index]
        window = padded[:, tap_index : tap_index + length, :].reshape(total_rows, columns)
        running = running + jnp.dot(window, tap_rows, preferred_element_type=jnp.float32)
    mixed = (activations.reshape(total_rows, channels).astype(jnp.float32) + running).astype(
        jnp.bfloat16
    )
    whole_mixed = lax.all_gather(mixed, "trk", axis=1, tiled=True)
    logits = jnp.dot(whole_mixed, head_weight, preferred_element_type=jnp.float32)
    tracks = jax.nn.softplus(logits + head_bias).astype(jnp.bfloat16)
    stride = straddle_map.shape[0]
    slot_ids = gene_slot.reshape(-1)
    onehot = (slot_ids[None, :] == jnp.arange(GENES_DEV + stride, dtype=jnp.int32)[:, None]).astype(
        jnp.bfloat16
    )
    slot_sums = jnp.dot(onehot, tracks, preferred_element_type=jnp.float32)
    counts = jnp.sum(onehot.astype(jnp.float32), axis=1)
    received, received_counts = passed_along((slot_sums[GENES_DEV:], counts[GENES_DEV:]), "pos", -1)
    owners = (straddle_map[:, None] == jnp.arange(GENES_DEV, dtype=jnp.int32)[None, :]).astype(
        jnp.float32
    )
    totals = slot_sums[:GENES_DEV] + jnp.dot(owners.T, received, precision=lax.Precision.HIGHEST)
    gene_counts = counts[:GENES_DEV] + jnp.dot(
        owners.T, received_counts, precision=lax.Precision.HIGHEST
    )
    gene_mean = totals / jnp.maximum(gene_counts, 1.0)[:, None]
    return (tracks.reshape(sequences, length, -1), gene_mean)


def solution(mesh):
    in_specs = (
        P(None, "pos", "trk"),
        P("trk"),
        P("trk"),
        P(None, None, "trk"),
        P(None, "trk"),
        P("trk"),
        P(None, "pos"),
        P("pos"),
    )
    out_specs = (P(None, "pos", "trk"), P("pos", "trk"))
    return jax.shard_map(
        per_device, mesh=mesh, in_specs=in_specs, out_specs=out_specs, check_vma=False
    )
```

profile of v0, /device:TPU:1, one launch (start us, length us, event | category | flops | bytes accessed | tf_op | source)
XLA Modules:
  0.0 220.8 jit_solution(16374574816708889458)
XLA Ops:
  7.2 1.5 fusion.10
  8.8 1.1 copy.25
  9.9 0.0 all-gather.5.cloned.1.call-start
  9.9 1.1 convert_bitcast_fusion
  11.0 0.1 copy.31
  11.1 82.5 %all-gather.3.cloned.1.call-done = bf16[4,512,1536]{1,0,2:T(4,128)(2,1)} async-done(((bf16[4,512,96]{1,0,2:T(4,128)(2,1)}), bf16[4,512,1536]{1,0,2:T(4,128)(2,1)}) %all-gather.3.cloned.1.call-update) | async-done | bytes 6291472 | tf_op jit(solution)/shard_map/all_gather | solution.py:41
  93.6 10.7 %copy.26 = bf16[4,512,1536]{2,1,0:T(8,128)(2,1)} copy(bf16[4,512,1536]{1,0,2:T(4,128)(2,1)} %all-gather.3.cloned.1.call-done) | data formatting | bytes 12582912 | tf_op jit(solution)/shard_map/all_gather | solution.py:41
  104.3 1.1 fusion.30
  105.5 3.9 %collective-permute-start = (bf16[4,1,1536]{2,1,0:T(2,128)(2,1)S(1)}, bf16[4,1,1536]{2,1,0:T(2,128)(2,1)S(1)}, u32[]{:S(2)}, u32[]{:S(2)}) collective-permute-start(bf16[4,1,1536]{2,1,0:T(2,128)(2,1)S(1)} %get-tuple-element.4), channel_id=1, source_target_pairs={{0,16},{16,32},{32,48},{48,64},{64,80},{80,96},{96,112},{112,128},... | collective-permute-start | bytes 36872 | tf_op jit(solution)/shard_map/ppermute | solution.py:17
  109.3 1.9 collective-permute-start.1
  111.3 4.8 %fusion.20 = f32[2048,96]{0,1:T(8,128)S(1)} fusion(bf16[2048,1536]{1,0:T(8,128)(2,1)} %bitcast.34, bf16[3,1536,96]{1,2,0:T(8,128)(2,1)S(1)} %copy-done.3), kind=kOutput, calls=%fused_computation.32 | convolution fusion | flops 603979776 | bytes 7372800 | tf_op jit(solution)/shard_map/dot_general | solution.py:48
  116.1 3.5 %pad_maximum_fusion.1 = (bf16[4,512,1536]{2,1,0:T(8,128)(2,1)S(1)}, bf16[4,512,1536]{2,1,0:T(8,128)(2,1)S(1)}) fusion(bf16[4,512,1536]{2,1,0:T(8,128)(2,1)S(1)} %copy-done.1, bf16[4,1,1536]{2,1,0:T(2,128)(2,1)S(1)} %collective-permute-done, bf16[4,1,1536]{2,1,0:T(2,128)(2,1)S(1)} %collective-permute-done.1), kind=kLoop, calls=%fused_computation.1 | loop fusion | flops 25165824 | bytes 18898944 | tf_op jit(solution)/shard_map/concatenate | solution.py:15
  119.6 2.0 fusion.18
  121.7 2.8 %fusion.2 = bf16[2048,96]{0,1:T(8,128)(2,1)} fusion(f32[2048,96]{0,1:T(8,128)S(1)} %bitcast.37, f32[2048,96]{0,1:T(8,128)S(1)} %fusion.18, f32[2048,96]{0,1:T(8,128)S(1)} %fusion.20, bf16[2048,1536]{1,0:T(8,128)(2,1)S(1)} %bitcast.35, bf16[3,1536,96]{1,2,0:T(8,128)(2,1)S(1)} %copy-done.3), kind=kOutput, calls=%fused_computation.7 | convolution fusion | flops 604766208 | bytes 9338880 | tf_op jit(solution)/shard_map/dot_general | solution.py:48
  124.5 0.1 convert_reduce_fusion
  124.7 0.1 slice.45
  124.8 2.0 collective-permute-start.3
  126.8 75.4 %all-gather.5.cloned.1.call-done = bf16[2048,1536]{0,1:T(8,128)(2,1)} async-done(((bf16[2048,96]{0,1:T(8,128)(2,1)}), bf16[2048,1536]{0,1:T(8,128)(2,1)}) %all-gather.5.cloned.1.call-update) | async-done | bytes 6291472 | tf_op jit(solution)/shard_map/all_gather | solution.py:52
  202.3 5.5 %fusion.3 = bf16[2048,256]{1,0:T(8,128)(2,1)S(1)} fusion(bf16[2048,1536]{0,1:T(8,128)(2,1)} %all-gather.5.cloned.1.call-done, bf16[1536,256]{1,0:T(8,128)(2,1)S(1)} %copy-done, f32[256]{0:T(256)S(1)} %copy-done.5), kind=kOutput, calls=%fused_computation.8 | convolution fusion | flops 1614807040 | bytes 8127488 | tf_op jit(solution)/shard_map/dot_general | solution.py:53
  207.8 0.3 fusion.17
  208.1 2.6 %collective-permute-start.2 = (f32[4,256]{1,0:T(4,128)S(1)}, f32[4,256]{1,0:T(4,128)S(1)}, u32[]{:S(2)}, u32[]{:S(2)}) collective-permute-start(f32[4,256]{1,0:T(4,128)S(1)} %slice.49), channel_id=1, source_target_pairs={{16,0},{32,16},{48,32},{64,48},{80,64},{96,80},{112,96},{128,112},... | collective-permute-start | bytes 12296 | tf_op jit(solution)/shard_map/ppermute | solution.py:29
  210.7 0.1 fusion.6
  210.8 2.3 %collective-permute-done.2 = f32[4,256]{1,0:T(4,128)S(1)} collective-permute-done((f32[4,256]{1,0:T(4,128)S(1)}, f32[4,256]{1,0:T(4,128)S(1)}, u32[]{:S(2)}, u32[]{:S(2)}) %collective-permute-start.2) | collective-permute-done | bytes 4128 | tf_op jit(solution)/shard_map/ppermute | solution.py:29
  213.1 0.9 fusion.4
  (22 shorter events, 0.1 us)
Async XLA Ops:
  7.2 195.1 %copy-start = (bf16[1536,256]{1,0:T(8,128)(2,1)S(1)}, bf16[1536,256]{1,0:T(8,128)(2,1)}, u32[]{:S(2)}) copy-start(bf16[1536,256]{1,0:T(8,128)(2,1)} %param.12) | copy-start | bytes 2359300
  7.2 86.4 %all-gather.3.cloned.1.call-start = ((), (), s32[]{:S(2)}) async-start(), calls=%async_computation | async-start | bytes 6684672 | tf_op jit(solution)/shard_map/all_gather | solution.py:41
  9.9 192.4 %all-gather.5.cloned.1.call-start = ((), (), s32[]{:S(2)}) async-start(), calls=%async_computation.1 | async-start | bytes 6684672 | tf_op jit(solution)/shard_map/all_gather | solution.py:52
  11.1 100.2 %copy-start.3 = (bf16[3,1536,96]{1,2,0:T(8,128)(2,1)S(1)}, bf16[3,1536,96]{1,2,0:T(8,128)(2,1)}, u32[]{:S(2)}) copy-start(bf16[3,1536,96]{1,2,0:T(8,128)(2,1)} %param.11) | copy-start | bytes 2654212
  104.3 11.8 %copy-start.1 = (bf16[4,512,1536]{2,1,0:T(8,128)(2,1)S(1)}, bf16[4,512,1536]{2,1,0:T(8,128)(2,1)}, u32[]{:S(2)}) copy-start(bf16[4,512,1536]{2,1,0:T(8,128)(2,1)} %copy.26) | copy-start | bytes 18874372
  105.5 10.6 %collective-permute-start = (bf16[4,1,1536]{2,1,0:T(2,128)(2,1)S(1)}, bf16[4,1,1536]{2,1,0:T(2,128)(2,1)S(1)}, u32[]{:S(2)}, u32[]{:S(2)}) collective-permute-start(bf16[4,1,1536]{2,1,0:T(2,128)(2,1)S(1)} %get-tuple-element.4), channel_id=1, source_target_pairs={{0,16},{16,32},{32,48},{48,64},{64,80},{80,96},{96,112},{112,128},... | collective-permute-start | bytes 36872 | tf_op jit(solution)/shard_map/ppermute | solution.py:17
  109.3 6.7 %collective-permute-start.1 = (bf16[4,1,1536]{2,1,0:T(2,128)(2,1)S(1)}, bf16[4,1,1536]{2,1,0:T(2,128)(2,1)S(1)}, u32[]{:S(2)}, u32[]{:S(2)}) collective-permute-start(bf16[4,1,1536]{2,1,0:T(2,128)(2,1)S(1)} %get-tuple-element.5), channel_id=1, source_target_pairs={{16,0},{32,16},{48,32},{64,48},{80,64},{96,80},{112,96},{128,112},... | collective-permute-start | bytes 36872 | tf_op jit(solution)/shard_map/ppermute | solution.py:19
  121.6 2.9 %copy-start.4 = (s32[4,512]{1,0:T(4,128)S(1)}, s32[4,512]{1,0:T(4,128)}, u32[]{:S(2)}) copy-start(s32[4,512]{1,0:T(4,128)} %param.14) | copy-start | bytes 24580
  121.6 80.6 %copy-start.5 = (f32[256]{0:T(256)S(1)}, f32[256]{0:T(256)}, u32[]{:S(2)}) copy-start(f32[256]{0:T(256)} %param.13) | copy-start | bytes 3076
  124.8 85.9 %copy-start.6 = (s32[4]{0:T(128)S(1)}, s32[4]{0:T(128)}, u32[]{:S(2)}) copy-start(s32[4]{0:T(128)} %param.15) | copy-start | bytes 52
  124.8 85.9 %collective-permute-start.3 = (f32[4]{0:T(128)S(1)}, f32[4]{0:T(128)S(1)}, u32[]{:S(2)}, u32[]{:S(2)}) collective-permute-start(f32[4]{0:T(128)S(1)} %slice.45), channel_id=1, source_target_pairs={{16,0},{32,16},{48,32},{64,48},{80,64},{96,80},{112,96},{128,112},... | collective-permute-start | bytes 56 | tf_op jit(solution)/shard_map/ppermute | solution.py:29
  207.8 6.2 %copy-start.2 = (bf16[2048,256]{1,0:T(8,128)(2,1)}, bf16[2048,256]{1,0:T(8,128)(2,1)S(1)}, u32[]{:S(2)}) copy-start(bf16[2048,256]{1,0:T(8,128)(2,1)S(1)} %fusion.3) | copy-start | bytes 3145732
  208.1 5.0 %collective-permute-start.2 = (f32[4,256]{1,0:T(4,128)S(1)}, f32[4,256]{1,0:T(4,128)S(1)}, u32[]{:S(2)}, u32[]{:S(2)}) collective-permute-start(f32[4,256]{1,0:T(4,128)S(1)} %slice.49), channel_id=1, source_target_pairs={{16,0},{32,16},{48,32},{64,48},{80,64},{96,80},{112,96},{128,112},... | collective-permute-start | bytes 12296 | tf_op jit(solution)/shard_map/ppermute | solution.py:29
Sparse Core Ops, SparseCore 0:
  11.6 81.9 all-gather.2
  124.6 77.5 all-gather.4
where the time goes:
time: 221 us
  waiting for transfers between devices  160 us (72%)
  matrix products  16.5 us (7%)
  between operations  14.2 us (6%)
  local copies, waits for them, and re-layouts  13.1 us (6%)
  starting transfers between devices  10.5 us (5%)
  other arithmetic  6.27 us (3%)
    all_gather x1, waiting for transfers between devices, per_device(): gathered = lax.all_gather(hidden, 'trk', axis=2, tiled=True)  82.5 us
    all_gather x1, waiting for transfers between devices, per_device(): whole_mixed = lax.all_gather(mixed, 'trk', axis=1, tiled=True)  75.4 us
    all_gather x1, local copies, waits for them, and re-layouts, per_device(): gathered = lax.all_gather(hidden, 'trk', axis=2, tiled=True)  10.7 us
    dot_general x3, matrix products, per_device(): jnp.dot(window, tap_rows, preferred_element_type=jnp.float32)  9.64 us
    dot_general x1, matrix products, per_device(): jnp.dot(whole_mixed, head_weight, preferred_element_type=jnp.float32)  5.54 us
    ppermute x2, starting transfers between devices, passed_along(): lax.ppermute(value, axis, [(source, source + steps) for source in range(i...  4.63 us
  transfers between devices with their start and end apart: 6, of which 3 were waited for; matrix products, arithmetic and copies ran while one was open for 5% of the time, Pallas kernels for 0%

commit v1 on v0

v1 whole, which is shorter than its diff:
```python
import functools

import jax
import jax.numpy as jnp
from jax import lax
from jax.experimental import pallas as pl
from jax.experimental.pallas import tpu as pltpu
from jax.sharding import PartitionSpec as P

MESH = pl.DeviceIdType.MESH
GENES_DEV = 32
STRAD = 4
SIDE = 4
BLK = 128


def kernel(
    n_pos, act, gain, bias, cw, hw, hb, gs, sm,
    tracks, gene_mean,
    raw, small, hid, cwb, hwb, prod, edge_out, edge_in, mix, out, acc, sums_in, strad_in, cnt_own, cnt_out, cnt_in, slots,
    send, recv, local,
):
    _, ch, length = act.shape
    group = SIDE * ch
    width = hb.shape[1]
    half = length // 2
    p = lax.axis_index("pos")
    t = lax.axis_index("trk")
    y, x = t // SIDE, t % SIDE

    def wrap(v, n):
        return lax.rem(v + n, n)

    def at_y(d):
        return wrap(y + d, SIDE)

    def at_x(d):
        return wrap(x + d, SIDE)

    def dev(dp=0, dy=0, dx=0):
        return (wrap(p + dp, n_pos), at_y(dy) * SIDE + at_x(dx))

    sibling = (p + 1 - 2 * lax.rem(p, 2), t)
    q = lax.rem(p, 4)
    q_z = lax.rem(q + 2, 4)
    q_s = q + 1 - 2 * lax.rem(q, 2)
    q_sz = lax.rem(q_s + 2, 4)

    used = [0, 0]
    started = []

    def remote(src, dst, device, landing):
        i = used[0]
        used[0] += 1
        copy = pltpu.make_async_remote_copy(
            src_ref=src, dst_ref=dst, send_sem=send.at[i], recv_sem=recv.at[i], device_id=device, device_id_type=MESH
        )
        copy.start()
        started.append(copy)
        return pltpu.make_async_remote_copy(
            src_ref=src, dst_ref=landing, send_sem=send.at[i], recv_sem=recv.at[i], device_id=device, device_id_type=MESH
        ).wait_recv

    def near(src, dst):
        i = used[1]
        used[1] += 1
        copy = pltpu.make_async_copy(src, dst, local.at[i])
        copy.start()
        return copy.wait

    partners = [dev(dy=d) for d in (1, 2, 3)] + [dev(dx=d) for d in (1, 2, 3)] + [dev(dp=d) for d in (1, -1, 2, -2)]
    partners += [dev(dp=s, dy=d) for s in (1, -1) for d in (1, 2, 3)]
    barrier = pltpu.get_barrier_semaphore()
    for partner in partners:
        pl.semaphore_signal(barrier, inc=1, device_id=partner, device_id_type=MESH)

    wait_own = [near(act.at[y, :, pl.ds(c * half, half)], raw.at[y, :, pl.ds(c * half, half)]) for c in range(2)]
    wait_cw = near(cw, cwb.at[:, y])
    wait_hw = [near(hw.at[:, k], hwb.at[y, k]) for k in range(SIDE)]
    small[y, :, :] = jnp.zeros(small.shape[1:], jnp.float32)
    small[y, 0:1, 0:ch] = gain[...]
    small[y, 1:2, 0:ch] = bias[...]
    small[y, 2:3, 0:width] = hb[...]
    rows = acc.shape[1]
    gene_ids = lax.broadcasted_iota(jnp.int32, (rows, length), 0)
    count = jnp.zeros((rows, 1), jnp.float32)
    for s in range(SIDE):
        count += jnp.sum((gs[s : s + 1, :] == gene_ids).astype(jnp.float32), axis=1, keepdims=True)
    count = jnp.broadcast_to(count, (rows, BLK))
    cnt_own[...] = count[:GENES_DEV]
    cnt_out[...] = count[GENES_DEV:]
    slots[...] = jnp.broadcast_to(gs[pl.ds(y, 1), :], slots.shape)
    pl.semaphore_wait(barrier, len(partners))

    wait_small = [remote(small.at[y], small.at[y], dev(dy=d), small.at[at_y(-d)]) for d in (1, 2, 3)]
    wait_raw = []
    for c in range(2):
        cols = pl.ds(c * half, half)
        wait_raw.append(
            [remote(act.at[at_y(d), :, cols], raw.at[y, :, cols], dev(dy=d), raw.at[at_y(-d), :, cols]) for d in (1, 2, 3)]
        )
    wait_cnt = remote(cnt_out, cnt_in, dev(dp=-1), cnt_in)

    def lanes(k):
        return pl.ds(pl.multiple_of(k * group, BLK), group)

    wait_cw1 = [
        remote(cw.at[:, :, lanes(q)], cwb.at[:, y, :, lanes(q)], dev(dy=d), cwb.at[:, at_y(-d), :, lanes(q)])
        for d in (1, 2, 3)
    ]

    wait_hid = []
    for w in wait_small:
        w()
    for c in range(2):
        cols = pl.ds(c * half, half)
        wait_own[c]()
        for w in wait_raw[c]:
            w()

        def activate(k, carry, cols=cols):
            vectors = jnp.transpose(small[k, :, 0:BLK])[0:ch]
            values = raw[k, :, cols].astype(jnp.float32) * vectors[:, 0:1] + vectors[:, 1:2]
            hid[k, x, :, cols] = jax.nn.gelu(values, approximate=True).astype(jnp.bfloat16)
            return carry

        lax.fori_loop(0, SIDE, activate, 0)
        wait_hid.append(
            [remote(hid.at[:, x, :, cols], hid.at[:, x, :, cols], dev(dx=d), hid.at[:, at_x(-d), :, cols]) for d in (1, 2, 3)]
        )

    low, high = pl.ds(0, ch // 2), pl.ds(ch // 2, ch // 2)
    wait_cw2, wait_cwz = [], []
    for d in (1, 2, 3):
        wait_cw1[d - 1]()
        k = at_y(-d)
        block = cwb.at[:, k, :, lanes(q)]
        wait_cwz.append(
            [
                remote(cwb.at[:, k, low, lanes(q)], cwb.at[:, k, low, lanes(q)], dev(dp=2), cwb.at[:, k, low, lanes(q_z)]),
                remote(cwb.at[:, k, high, lanes(q)], cwb.at[:, k, high, lanes(q)], dev(dp=-2), cwb.at[:, k, high, lanes(q_z)]),
            ]
        )
        wait_cw2.append(remote(block, block, sibling, cwb.at[:, k, :, lanes(q_s)]))
    wait_hw1 = [remote(hw.at[:, q], hwb.at[y, q], dev(dy=d), hwb.at[at_y(-d), q]) for d in (1, 2, 3)]
    for d in (1, 2, 3):
        k = at_y(-d)
        for w, part in zip(wait_cwz[d - 1], (low, high)):
            w()
            block = cwb.at[:, k, part, lanes(q_z)]
            wait_cw2.append(remote(block, block, sibling, cwb.at[:, k, part, lanes(q_sz)]))
    for w in wait_cw2:
        w()
    wait_cw()

    def products(c):
        cols = pl.ds(c * half, half)

        def tap(k, carry):
            prod[k, :, cols] = jnp.dot(
                cwb[k].reshape(group, SIDE * group),
                hid[:, :, :, cols].reshape(SIDE * group, half),
                preferred_element_type=jnp.float32,
            )
            return carry

        lax.fori_loop(0, 3, tap, 0)

    for w in wait_hid[0]:
        w()
    products(0)
    edge_out[1] = jnp.transpose(prod[2, :, 0:BLK])[0:8]
    wait_right = remote(edge_out.at[1], edge_in.at[1], dev(dp=-1), edge_in.at[1])

    first, last = pl.ds(0, SIDE // 2), pl.ds(SIDE // 2, SIDE // 2)
    wait_hw2, wait_hwz = [], []
    for d in (1, 2, 3):
        wait_hw1[d - 1]()
        k = at_y(-d)
        wait_hwz.append(
            [
                remote(hwb.at[k, q, first], hwb.at[k, q, first], dev(dp=2), hwb.at[k, q_z, first]),
                remote(hwb.at[k, q, last], hwb.at[k, q, last], dev(dp=-2), hwb.at[k, q_z, last]),
            ]
        )
        wait_hw2.append(remote(hwb.at[k, q], hwb.at[k, q], sibling, hwb.at[k, q_s]))

    for w in wait_hid[1]:
        w()
    products(1)
    edge_out[0] = jnp.transpose(prod[0, :, length - BLK : length])[BLK - 8 : BLK]
    wait_left = remote(edge_out.at[0], edge_in.at[0], dev(dp=1), edge_in.at[0])

    wait_mix = []
    lane = lax.broadcasted_iota(jnp.int32, (group, BLK), 1)
    row = lax.broadcasted_iota(jnp.int32, (BLK, group), 0)
    blocks = length // BLK
    order = list(range(1, blocks)) + [0]
    for b in order:
        here = slice(b * BLK, (b + 1) * BLK)
        before = pltpu.roll(prod[0, :, here], 1, 1)
        if b > 0:
            other = pltpu.roll(prod[0, :, (b - 1) * BLK : b * BLK], 1, 1)
        else:
            other = jnp.zeros_like(before)
        total = prod[1, :, here] + jnp.where(lane == 0, other, before)
        after = pltpu.roll(prod[2, :, here], BLK - 1, 1)
        if b < blocks - 1:
            other = pltpu.roll(prod[2, :, (b + 1) * BLK : (b + 2) * BLK], BLK - 1, 1)
        else:
            other = jnp.zeros_like(after)
        total += jnp.where(lane == BLK - 1, other, after)
        total += raw[:, :, here].reshape(group, BLK).astype(jnp.float32)
        total = jnp.transpose(total)
        if b == 0:
            wait_left()
            total += jnp.where((row == 0) & (p > 0), edge_in[0, 7:8, :], 0.0)
        if b == blocks - 1:
            wait_right()
            total += jnp.where((row == BLK - 1) & (p < n_pos - 1), edge_in[1, 0:1, :], 0.0)
        mix[here, lanes(x)] = total.astype(jnp.bfloat16)
        block = mix.at[pl.ds(b * BLK, BLK), lanes(x)]
        wait_mix.append(
            [remote(block, block, dev(dx=d), mix.at[pl.ds(b * BLK, BLK), lanes(at_x(-d))]) for d in (1, 2, 3)]
        )

    for d in (1, 2, 3):
        k = at_y(-d)
        for w, part in zip(wait_hwz[d - 1], (first, last)):
            w()
            wait_hw2.append(remote(hwb.at[k, q_z, part], hwb.at[k, q_z, part], sibling, hwb.at[k, q_sz, part]))
    for w in wait_hw2 + wait_hw:
        w()

    acc[...] = jnp.zeros_like(acc)
    wait_out = []
    for b, waits in zip(order, wait_mix):
        here = slice(b * BLK, (b + 1) * BLK)
        for w in waits:
            w()
        onehot = (slots[0:1, here] == lax.broadcasted_iota(jnp.int32, (rows, BLK), 0)).astype(jnp.bfloat16)
        for d in (1, 2, 3, 0):
            k = at_y(d)
            logits = jnp.dot(
                mix[here, :], hwb[k].reshape(SIDE * group, width), preferred_element_type=jnp.float32
            )
            logits += small[k, 2:3, 0:width]
            values = (jnp.maximum(logits, 0.0) + jnp.log1p(jnp.exp(-jnp.abs(logits)))).astype(jnp.bfloat16)
            out[d, here, :] = values
            acc[d] += jnp.dot(onehot, values, preferred_element_type=jnp.float32)
            spot = pl.ds(b * BLK, BLK)
            if d:
                wait_out.append(
                    remote(out.at[d, spot], tracks.at[y, spot], dev(dy=d), tracks.at[at_y(-d), spot])
                )
            else:
                wait_out.append(near(out.at[0, spot], tracks.at[y, spot]))

    own, tail = pl.ds(0, GENES_DEV), pl.ds(GENES_DEV, rows - GENES_DEV)
    wait_sums = [
        remote(acc.at[d, tail], strad_in.at[y], dev(dp=-1, dy=d), strad_in.at[at_y(-d)]) for d in range(SIDE)
    ]
    wait_sums += [remote(acc.at[d, own], sums_in.at[y], dev(dy=d), sums_in.at[at_y(-d)]) for d in (1, 2, 3)]
    wait_cnt()
    for w in wait_sums:
        w()
    totals = acc[0, 0:GENES_DEV, :]
    for d in (1, 2, 3):
        totals += sums_in[at_y(-d)]
    strays = strad_in[0] + strad_in[1] + strad_in[2] + strad_in[3]
    counts = cnt_own[...]
    gene = lax.broadcasted_iota(jnp.int32, (GENES_DEV, width), 0)
    for s in range(STRAD):
        totals += jnp.where(gene == sm[s], strays[s : s + 1, :], 0.0)
        counts += jnp.where(gene[:, 0:BLK] == sm[s], cnt_in[s : s + 1, :], 0.0)
    gene_mean[...] = totals / jnp.maximum(counts, 1.0)[:, 0:1]
    for w in wait_out:
        w()
    for copy in started:
        copy.wait_send()


def solution(mesh):
    n_pos = mesh.shape["pos"]

    def per_device(act, gain, bias, cw, hw, hb, gs, sm):
        seqs, length, ch = act.shape
        group = SIDE * ch
        width = hw.shape[1]
        rows = GENES_DEV + 8
        f32, bf16 = jnp.float32, jnp.bfloat16
        anywhere = pl.BlockSpec(memory_space=pl.ANY)
        vmem = pl.BlockSpec(memory_space=pltpu.VMEM)
        tracks, gene_mean = pl.pallas_call(
            functools.partial(kernel, n_pos),
            name="fused_block",
            out_shape=(
                jax.ShapeDtypeStruct((seqs, length, width), bf16),
                jax.ShapeDtypeStruct((GENES_DEV, width), f32),
            ),
            in_specs=[
                anywhere, vmem, vmem, anywhere, anywhere, vmem, vmem,
                pl.BlockSpec(memory_space=pltpu.SMEM),
            ],
            out_specs=(anywhere, vmem),
            scratch_shapes=[
                pltpu.VMEM((SIDE, ch, length), bf16),
                pltpu.VMEM((SIDE, 8, 256), f32),
                pltpu.VMEM((SIDE, SIDE, ch, length), bf16),
                pltpu.VMEM((3, SIDE, ch, SIDE * group), bf16),
                pltpu.VMEM((SIDE, SIDE, SIDE, ch, width), bf16),
                pltpu.VMEM((3, group, length), f32),
                pltpu.VMEM((2, 8, group), f32),
                pltpu.VMEM((2, 8, group), f32),
                pltpu.VMEM((length, SIDE * group), bf16),
                pltpu.VMEM((SIDE, length, width), bf16),
                pltpu.VMEM((SIDE, rows, width), f32),
                pltpu.VMEM((SIDE, GENES_DEV, width), f32),
                pltpu.VMEM((SIDE, 8, width), f32),
                pltpu.VMEM((GENES_DEV, BLK), f32),
                pltpu.VMEM((8, BLK), f32),
                pltpu.VMEM((8, BLK), f32),
                pltpu.VMEM((8, length), jnp.int32),
                pltpu.SemaphoreType.DMA((96,)),
                pltpu.SemaphoreType.DMA((96,)),
                pltpu.SemaphoreType.DMA((16,)),
            ],
            compiler_params=pltpu.CompilerParams(
                collective_id=0, has_side_effects=True, vmem_limit_bytes=48 * 2**20
            ),
        )(
            jnp.transpose(act, (0, 2, 1)),
            gain.reshape(1, ch),
            bias.reshape(1, ch),
            jnp.transpose(cw, (0, 2, 1)),
            hw.reshape(SIDE, SIDE, ch, width),
            hb.reshape(1, width),
            gs,
            sm,
        )
        return tracks, gene_mean

    in_specs = (
        P(None, "pos", "trk"),
        P("trk"),
        P("trk"),
        P(None, None, "trk"),
        P(None, "trk"),
        P("trk"),
        P(None, "pos"),
        P("pos"),
    )
    out_specs = (P(None, "pos", "trk"), P("pos", "trk"))
    return jax.shard_map(per_device, mesh=mesh, in_specs=in_specs, out_specs=out_specs, check_vma=False)
```

time: 221 us -> 78.8 us (0.36)
  waiting for transfers between devices: 160 us -> 0 us
  Pallas kernels: 0 us -> 72.3 us
  matrix products: 16.5 us -> 0 us
  between operations: 14.2 us -> 0.69 us
  starting transfers between devices: 10.5 us -> 0 us
  local copies, waits for them, and re-layouts: 13.1 us -> 5.57 us
  other arithmetic: 6.27 us -> 0 us
    all_gather x2 -> x0, waiting for transfers between devices: 158 us -> none  [the longest x1 82.5 us: per_device(): gathered = lax.all_gather(hidden, 'trk', axis=2, tiled=True)]
    pallas_call x0 -> x1, Pallas kernels: none -> 72.3 us  [per_device(): pl.pallas_call(functools.partial(kernel, n_pos), name='fused_block', out_...]
    dot_general x7 -> x0, matrix products: 16.5 us -> none  [the longest x3 9.64 us: per_device(): jnp.dot(window, tap_rows, preferred_element_type=jnp.float32)]
    all_gather x1 -> x0, local copies, waits for them, and re-layouts: 10.7 us -> none  [per_device(): gathered = lax.all_gather(hidden, 'trk', axis=2, tiled=True)]
    ppermute x4 -> x0, starting transfers between devices: 10.4 us -> none  [the longest x2 4.63 us: passed_along(): lax.ppermute(value, axis, [(source, source + steps) for source in range(i...]
    unnamed x15 -> x18, local copies, waits for them, and re-layouts: 0.05 us -> 5.57 us
    concatenate x1 -> x0, other arithmetic: 3.5 us -> none  [with_halo(): jnp.concatenate([lax.ppermute(tail, axis, [(i, (i + 1) % count) for i in...]
    ppermute x4 -> x0, waiting for transfers between devices: 2.3 us -> none  [the longest x2 2.29 us: passed_along(): lax.ppermute(value, axis, [(source, source + steps) for source in range(i...]
  transfers between devices with their start and end apart: 6 -> 0, of which waited for: 3 -> 0; matrix products, arithmetic and copies ran while one was open for 5% -> 0% of each run, Pallas kernels for 0% -> 0%
where the time goes in v1:
time: 78.8 us; the launch traced here: 78.6 us
  Pallas kernels  72.3 us (92%)
  local copies, waits for them, and re-layouts  5.57 us (7%)
    pallas_call x1, Pallas kernels, per_device(): pl.pallas_call(functools.partial(kernel, n_pos), name='fused_block', out_...  72.3 us
    unnamed x18, local copies, waits for them, and re-layouts  5.57 us

profile of v1, /device:TPU:1, one launch (start us, length us, event | category | flops | bytes accessed | tf_op | source)
XLA Modules:
  0.0 78.6 jit_solution(3729117132209770961)
XLA Ops:
  0.6 0.0 copy-start.3
  0.6 0.0 copy-start.6
  0.7 0.0 copy-start.7
  0.7 0.0 copy-start.4
  0.7 0.0 copy-start.5
  0.7 0.6 copy-done.3
  1.3 0.0 copy-done.6
  1.3 0.0 copy-done.7
  1.3 0.0 copy-done.4
  1.4 0.0 copy-done.5
  1.4 0.0 copy-start
  1.4 1.2 %copy-done = bf16[3,1536,96]{1,2,0:T(8,128)(2,1)S(1)} copy-done((bf16[3,1536,96]{1,2,0:T(8,128)(2,1)S(1)}, bf16[3,1536,96]{1,2,0:T(8,128)(2,1)}, u32[]{:S(2)}) %copy-start) | copy-done | bytes 884760
  2.5 0.0 copy-start.1
  2.5 1.1 %copy-done.1 = bf16[1536,256]{1,0:T(8,128)(2,1)S(1)} copy-done((bf16[1536,256]{1,0:T(8,128)(2,1)S(1)}, bf16[1536,256]{1,0:T(8,128)(2,1)}, u32[]{:S(2)}) %copy-start.1) | copy-done | bytes 786456
  3.7 0.0 copy-start.2
  3.7 1.0 %copy-done.2 = bf16[4,512,96]{1,2,0:T(8,128)(2,1)S(1)} copy-done((bf16[4,512,96]{1,2,0:T(8,128)(2,1)S(1)}, bf16[4,512,96]{1,2,0:T(8,128)(2,1)}, u32[]{:S(2)}) %copy-start.2) | copy-done | bytes 393240
  4.7 72.3 %fused_block.1 = (bf16[4,512,256]{2,1,0:T(8,128)(2,1)S(1)}, f32[32,256]{1,0:T(8,128)S(1)}) custom-call(bf16[4,96,512]{2,1,0:T(8,128)(2,1)S(1)} %bitcast.8, f32[1,96]{1,0:T(1,128)S(1)} %bitcast.10, f32[1,96]{1,0:T(1,128)S(1)} %bitcast.11, bf16[3,96,1536]{2,1,0:T(8,128)(2,1)S(1)} %bitcast.6, bf16[4,4,96,256]{3,2,1,0:T(8,128)(2,1)S(1)} %bitcast.7, ...), custom_call_target="tpu_custom_call" | custom-call | tf_op jit(solution)/shard_map/fused_block/pallas_call | solution.py:294
  77.0 1.0 %copy.12 = bf16[4,512,256]{2,1,0:T(8,128)(2,1)} copy(bf16[4,512,256]{2,1,0:T(8,128)(2,1)S(1)} %get-tuple-element.4) | data formatting | bytes 2097152
  78.0 0.6 copy.13
Async XLA Ops:
  0.6 0.7 copy-start.3
  0.6 0.7 copy-start.6
  0.7 0.7 copy-start.7
  0.7 0.7 copy-start.4
  0.7 0.7 copy-start.5
  1.4 1.2 %copy-start = (bf16[3,1536,96]{1,2,0:T(8,128)(2,1)S(1)}, bf16[3,1536,96]{1,2,0:T(8,128)(2,1)}, u32[]{:S(2)}) copy-start(bf16[3,1536,96]{1,2,0:T(8,128)(2,1)} %param.11) | copy-start | bytes 2654212
  2.5 1.1 %copy-start.1 = (bf16[1536,256]{1,0:T(8,128)(2,1)S(1)}, bf16[1536,256]{1,0:T(8,128)(2,1)}, u32[]{:S(2)}) copy-start(bf16[1536,256]{1,0:T(8,128)(2,1)} %param.12) | copy-start | bytes 2359300
  3.7 1.0 %copy-start.2 = (bf16[4,512,96]{1,2,0:T(8,128)(2,1)S(1)}, bf16[4,512,96]{1,2,0:T(8,128)(2,1)}, u32[]{:S(2)}) copy-start(bf16[4,512,96]{1,2,0:T(8,128)(2,1)} %param.8) | copy-start | bytes 1179652

commit v2 on v1

v2 whole, which is shorter than its diff:
```python
import functools

import jax
import jax.numpy as jnp
from jax import lax
from jax.experimental import pallas as pl
from jax.experimental.pallas import tpu as pltpu
from jax.sharding import PartitionSpec as P

MESH = pl.DeviceIdType.MESH
GENES_DEV = 32
STRAD = 4
SIDE = 4
BLK = 128


def kernel(
    n_pos, act, gain, bias, cw, hw, hb, gs, sm,
    tracks, gene_mean,
    gain_v, bias_v, hb_v, gs_v, sm_v, raw, small, hid, cwb, hwb, prod, edge_out, edge_in, mix, out, acc, sums_in, strad_in, cnt_own, cnt_out, cnt_in, slots,
    send, recv, local,
):
    _, ch, length = act.shape
    group = SIDE * ch
    width = hb.shape[1]
    half = length // 2
    p = lax.axis_index("pos")
    t = lax.axis_index("trk")
    y, x = t // SIDE, t % SIDE

    def wrap(v, n):
        return lax.rem(v + n, n)

    def at_y(d):
        return wrap(y + d, SIDE)

    def at_x(d):
        return wrap(x + d, SIDE)

    def dev(dp=0, dy=0, dx=0):
        return (wrap(p + dp, n_pos), at_y(dy) * SIDE + at_x(dx))

    sibling = (p + 1 - 2 * lax.rem(p, 2), t)
    q = lax.rem(p, 4)
    q_z = lax.rem(q + 2, 4)
    q_s = q + 1 - 2 * lax.rem(q, 2)
    q_sz = lax.rem(q_s + 2, 4)

    used = [0, 0]
    started = []

    pending = []

    def once(wait):
        done = []

        def call():
            if not done:
                done.append(True)
                wait()

        pending.append(call)
        return call

    def finish():
        for w in pending:
            w()
        for copy in started:
            copy.wait_send()

    def remote(src, dst, device, landing):
        i = used[0]
        used[0] += 1
        copy = pltpu.make_async_remote_copy(
            src_ref=src, dst_ref=dst, send_sem=send.at[i], recv_sem=recv.at[i], device_id=device, device_id_type=MESH
        )
        copy.start()
        started.append(copy)
        arrival = pltpu.make_async_remote_copy(
            src_ref=src, dst_ref=landing, send_sem=send.at[i], recv_sem=recv.at[i], device_id=device, device_id_type=MESH
        )
        return once(arrival.wait_recv)

    def near(src, dst):
        i = used[1]
        used[1] += 1
        copy = pltpu.make_async_copy(src, dst, local.at[i])
        copy.start()
        return once(copy.wait)

    partners = [dev(dy=d) for d in (1, 2, 3)] + [dev(dx=d) for d in (1, 2, 3)] + [dev(dp=d) for d in (1, -1, 2, -2)]
    partners += [dev(dp=s, dy=d) for s in (1, -1) for d in (1, 2, 3)]
    barrier = pltpu.get_barrier_semaphore()
    for partner in partners:
        pl.semaphore_signal(barrier, inc=1, device_id=partner, device_id_type=MESH)

    wait_own = [near(act.at[y, :, pl.ds(c * half, half)], raw.at[y, :, pl.ds(c * half, half)]) for c in range(2)]
    wait_vectors = [near(*pair) for pair in ((gain, gain_v), (bias, bias_v), (hb, hb_v), (gs, gs_v), (sm, sm_v))]
    wait_cw = near(cw, cwb.at[:, y])
    wait_hw = [near(hw.at[:, k], hwb.at[y, k]) for k in range(SIDE)]
    small[y, :, :] = jnp.zeros(small.shape[1:], jnp.float32)
    for w in wait_vectors:
        w()
    small[y, 0:1, 0:ch] = gain_v[...]
    small[y, 1:2, 0:ch] = bias_v[...]
    small[y, 2:3, 0:width] = hb_v[...]
    pl.semaphore_wait(barrier, len(partners))

    wait_small = [remote(small.at[y], small.at[y], dev(dy=d), small.at[at_y(-d)]) for d in (1, 2, 3)]

    def raw_to_column(c):
        cols = pl.ds(c * half, half)
        return [
            remote(act.at[at_y(d), :, cols], raw.at[y, :, cols], dev(dy=d), raw.at[at_y(-d), :, cols]) for d in (1, 2, 3)
        ]

    def ring_first(view, spots, up, down):
        mine = view(spots[0], None)
        return remote(mine, mine, up, view(spots[1], None)), remote(mine, mine, down, view(spots[2], None))

    def ring_second(view, spots, up, down, waits):
        waits[0]()
        block = view(spots[1], 0)
        low = remote(block, block, up, view(spots[3], 0))
        waits[1]()
        block = view(spots[2], 1)
        high = remote(block, block, down, view(spots[3], 1))
        return low, high

    spots_y = (y, at_y(-1), at_y(1), at_y(2))
    spots_x = (x, at_x(-1), at_x(1), at_x(2))
    up_y, down_y, up_x, down_x = dev(dy=1), dev(dy=-1), dev(dx=1), dev(dx=-1)
    above, below = dev(dp=2), dev(dp=-2)

    def lanes(k):
        return pl.ds(pl.multiple_of(k * group, BLK), group)

    def cw_view(tap):
        def of(quarter):
            def view(k, part):
                if part is None:
                    return cwb.at[tap, k, :, lanes(quarter)]
                return cwb.at[tap, k, pl.ds(part * (ch // 2), ch // 2), lanes(quarter)]

            return view

        return of

    def hw_view(quarter):
        def view(k, part):
            if part is None:
                return hwb.at[k, quarter]
            return hwb.at[k, quarter, pl.ds(part * (SIDE // 2), SIDE // 2)]

        return view

    def to_z(view, k):
        return [
            remote(view(q)(k, 0), view(q)(k, 0), above, view(q_z)(k, 0)),
            remote(view(q)(k, 1), view(q)(k, 1), below, view(q_z)(k, 1)),
        ]

    def to_sibling(view, k, part, mine, theirs):
        return remote(view(mine)(k, part), view(mine)(k, part), sibling, view(theirs)(k, part))

    def weights_second(view, ring):
        opposite = ring_second(view(q), spots_y, up_y, down_y, ring)
        from_z, from_sibling = [], []
        for k in spots_y[1:3]:
            from_z += to_z(view, k)
            from_sibling.append(to_sibling(view, k, None, q, q_s))
        return opposite, from_z, from_sibling

    def weights_third(view, opposite, from_z, from_sibling):
        for w in opposite:
            w()
        from_z += to_z(view, spots_y[3])
        from_sibling.append(to_sibling(view, spots_y[3], None, q, q_s))

    def weights_fourth(view, from_z, from_sibling, which):
        for i in which:
            from_z[2 * i]()
            from_z[2 * i + 1]()
            from_sibling.append(to_sibling(view, spots_y[1 + i], None, q_z, q_sz))

    def hid_view(c):
        def view(k, part):
            if part is None:
                return hid.at[:, k, :, pl.ds(c * half, half)]
            return hid.at[pl.ds(part * (SIDE // 2), SIDE // 2), k, :, pl.ds(c * half, half)]

        return view

    def activate(c):
        cols = pl.ds(c * half, half)
        wait_own[c]()
        for w in wait_raw[c]:
            w()

        def channels(k, carry):
            vectors = jnp.transpose(small[k, :, 0:BLK])[0:ch]
            values = raw[k, :, cols].astype(jnp.float32) * vectors[:, 0:1] + vectors[:, 1:2]
            hid[k, x, :, cols] = jax.nn.gelu(values, approximate=True).astype(jnp.bfloat16)
            return carry

        lax.fori_loop(0, SIDE, channels, 0)
        return ring_first(hid_view(c), spots_x, up_x, down_x)

    taps = range(3)
    cw_of = [cw_view(tap) for tap in taps]
    wait_raw = [raw_to_column(0)]
    wait_cw()
    cw_ring = [ring_first(cw_of[0](q), spots_y, up_y, down_y)]
    wait_raw.append(raw_to_column(1))
    for tap in (1, 2):
        cw_ring.append(ring_first(cw_of[tap](q), spots_y, up_y, down_y))

    rows = acc.shape[1]
    gene_ids = lax.broadcasted_iota(jnp.int32, (rows, length), 0)
    count = jnp.zeros((rows, 1), jnp.float32)
    for s in range(SIDE):
        count += jnp.sum((gs_v[s : s + 1, :] == gene_ids).astype(jnp.float32), axis=1, keepdims=True)
    count = jnp.broadcast_to(count, (rows, BLK))
    cnt_own[...] = count[:GENES_DEV]
    cnt_out[...] = count[GENES_DEV:]
    slots[...] = jnp.broadcast_to(gs_v[pl.ds(y, 1), :], slots.shape)
    wait_cnt = remote(cnt_out, cnt_in, dev(dp=-1), cnt_in)

    for w in wait_small:
        w()
    hid_ring = [activate(0)]
    cw_parts = [weights_second(cw_of[0], cw_ring[0])]
    hid_ring.append(activate(1))
    cw_parts.append(weights_second(cw_of[1], cw_ring[1]))
    cw_parts.append(weights_second(cw_of[2], cw_ring[2]))
    for w in wait_hw:
        w()
    hw_ring = ring_first(hw_view(q), spots_y, up_y, down_y)
    weights_fourth(cw_of[0], *cw_parts[0][1:], (0, 1))
    weights_third(cw_of[0], *cw_parts[0])
    hid_far = [ring_second(hid_view(0), spots_x, up_x, down_x, hid_ring[0])]
    weights_third(cw_of[1], *cw_parts[1])
    weights_third(cw_of[2], *cw_parts[2])
    weights_fourth(cw_of[1], *cw_parts[1][1:], (0, 1))
    weights_fourth(cw_of[2], *cw_parts[2][1:], (0, 1))
    weights_fourth(cw_of[0], *cw_parts[0][1:], (2,))
    hid_far.append(ring_second(hid_view(1), spots_x, up_x, down_x, hid_ring[1]))
    weights_fourth(cw_of[1], *cw_parts[1][1:], (2,))
    weights_fourth(cw_of[2], *cw_parts[2][1:], (2,))

    def product(tap, c):
        cols = pl.ds(c * half, half)
        for w in (*cw_parts[tap][2], *hid_far[c]):
            w()
        prod[tap, :, cols] = jnp.dot(
            cwb[tap].reshape(group, SIDE * group),
            hid[:, :, :, cols].reshape(SIDE * group, half),
            preferred_element_type=jnp.float32,
        )

    product(0, 0)
    product(1, 0)
    hw_parts = weights_second(hw_view, hw_ring)
    product(2, 0)
    edge_out[1] = jnp.transpose(prod[2, :, 0:BLK])[0:8]
    wait_right = remote(edge_out.at[1], edge_in.at[1], dev(dp=-1), edge_in.at[1])
    product(2, 1)

    def mix_view(first, size):
        def view(k, part):
            if part is None:
                return mix.at[pl.ds(first, size), lanes(k)]
            return mix.at[pl.ds(first + part * (size // 2), size // 2), lanes(k)]

        return view

    lane = lax.broadcasted_iota(jnp.int32, (group, BLK), 1)
    row = lax.broadcasted_iota(jnp.int32, (BLK, group), 0)
    blocks = length // BLK
    pieces = [(b * BLK, BLK) for b in range(1, blocks)] + [(0, BLK // 2), (BLK // 2, BLK // 2)]

    def mixed(b):
        here = slice(b * BLK, (b + 1) * BLK)
        before = pltpu.roll(prod[0, :, here], 1, 1)
        if b > 0:
            other = pltpu.roll(prod[0, :, (b - 1) * BLK : b * BLK], 1, 1)
        else:
            other = jnp.zeros_like(before)
        total = prod[1, :, here] + jnp.where(lane == 0, other, before)
        after = pltpu.roll(prod[2, :, here], BLK - 1, 1)
        if b < blocks - 1:
            other = pltpu.roll(prod[2, :, (b + 1) * BLK : (b + 2) * BLK], BLK - 1, 1)
        else:
            other = jnp.zeros_like(after)
        total += jnp.where(lane == BLK - 1, other, after)
        total += raw[:, :, here].reshape(group, BLK).astype(jnp.float32)
        total = jnp.transpose(total)
        if b == 0:
            wait_left()
            total += jnp.where((row == 0) & (p > 0), edge_in[0, 7:8, :], 0.0)
        if b == blocks - 1:
            wait_right()
            total += jnp.where((row == BLK - 1) & (p < n_pos - 1), edge_in[1, 0:1, :], 0.0)
        mix[here, lanes(x)] = total.astype(jnp.bfloat16)

    own, tail = pl.ds(0, GENES_DEV), pl.ds(GENES_DEV, rows - GENES_DEV)
    wait_sums = []

    def head(first, size, final):
        here = slice(first, first + size)
        spot = pl.ds(first, size)
        onehot = (slots[0:1, here] == lax.broadcasted_iota(jnp.int32, (rows, size), 0)).astype(jnp.bfloat16)
        for d in (2, 1, 3, 0):
            k = at_y(d)
            logits = jnp.dot(
                mix[here, :], hwb[k].reshape(SIDE * group, width), preferred_element_type=jnp.float32
            )
            logits += small[k, 2:3, 0:width]
            values = (jnp.maximum(logits, 0.0) + jnp.log1p(jnp.exp(-jnp.abs(logits)))).astype(jnp.bfloat16)
            out[d, here, :] = values
            acc[d] += jnp.dot(onehot, values, preferred_element_type=jnp.float32)
            if final:
                wait_sums.append(remote(acc.at[d, tail], strad_in.at[y], dev(dp=-1, dy=d), strad_in.at[at_y(-d)]))
                if d:
                    wait_sums.append(remote(acc.at[d, own], sums_in.at[y], dev(dy=d), sums_in.at[at_y(-d)]))
            if d:
                remote(out.at[d, spot], tracks.at[y, spot], dev(dy=d), tracks.at[at_y(-d), spot])
            else:
                near(out.at[0, spot], tracks.at[y, spot])

    mix_ring, mix_far = [], []

    def mix_first(i):
        mix_ring.append(ring_first(mix_view(*pieces[i]), spots_x, up_x, down_x))

    def mix_second(i):
        mix_far.append(ring_second(mix_view(*pieces[i]), spots_x, up_x, down_x, mix_ring[i]))

    mixed(1)
    mix_first(0)
    acc[...] = jnp.zeros_like(acc)
    product(0, 1)
    edge_out[0] = jnp.transpose(prod[0, :, length - BLK : length])[BLK - 8 : BLK]
    wait_left = remote(edge_out.at[0], edge_in.at[0], dev(dp=1), edge_in.at[0])
    product(1, 1)
    mixed(2)
    mix_first(1)
    weights_third(hw_view, *hw_parts)
    mixed(3)
    mix_second(0)
    mix_first(2)
    weights_fourth(hw_view, *hw_parts[1:], (0, 1))
    mixed(0)
    mix_second(1)
    mix_first(3)
    mix_first(4)
    weights_fourth(hw_view, *hw_parts[1:], (2,))
    for w in hw_parts[2]:
        w()
    for i, piece in enumerate(pieces):
        for w in mix_far[i]:
            w()
        head(*piece, i == len(pieces) - 1)
        if i + 2 < len(pieces):
            mix_second(i + 2)

    wait_cnt()
    for w in wait_sums:
        w()
    totals = acc[0, 0:GENES_DEV, :]
    for d in (1, 2, 3):
        totals += sums_in[at_y(-d)]
    strays = strad_in[0] + strad_in[1] + strad_in[2] + strad_in[3]
    counts = cnt_own[...]
    gene = lax.broadcasted_iota(jnp.int32, (GENES_DEV, width), 0)
    for s in range(STRAD):
        totals += jnp.where(gene == sm_v[0:1, s : s + 1], strays[s : s + 1, :], 0.0)
        counts += jnp.where(gene[:, 0:BLK] == sm_v[0:1, s : s + 1], cnt_in[s : s + 1, :], 0.0)
    gene_mean[...] = totals / jnp.maximum(counts, 1.0)[:, 0:1]
    finish()


def solution(mesh):
    n_pos = mesh.shape["pos"]

    def per_device(act, gain, bias, cw, hw, hb, gs, sm):
        seqs, length, ch = act.shape
        group = SIDE * ch
        width = hw.shape[1]
        rows = GENES_DEV + 8
        f32, bf16 = jnp.float32, jnp.bfloat16
        anywhere = pl.BlockSpec(memory_space=pl.ANY)
        hbm = pl.BlockSpec(memory_space=pltpu.HBM)
        vmem = pl.BlockSpec(memory_space=pltpu.VMEM)
        operands = (
            jnp.transpose(act, (0, 2, 1)),
            gain.reshape(1, ch),
            bias.reshape(1, ch),
            jnp.transpose(cw, (0, 2, 1)),
            hw.reshape(SIDE, SIDE, ch, width),
            hb.reshape(1, width),
            gs,
            sm.reshape(1, STRAD),
        )
        tracks, gene_mean = pl.pallas_call(
            functools.partial(kernel, n_pos),
            name="fused_block",
            out_shape=(
                pltpu.VMEM((seqs, length, width), bf16),
                jax.ShapeDtypeStruct((GENES_DEV, width), f32),
            ),
            in_specs=[hbm] * 8,
            out_specs=(anywhere, vmem),
            scratch_shapes=[
                pltpu.VMEM((1, ch), f32),
                pltpu.VMEM((1, ch), f32),
                pltpu.VMEM((1, width), f32),
                pltpu.VMEM((seqs, length), jnp.int32),
                pltpu.VMEM((1, STRAD), jnp.int32),
                pltpu.VMEM((SIDE, ch, length), bf16),
                pltpu.VMEM((SIDE, 8, 256), f32),
                pltpu.VMEM((SIDE, SIDE, ch, length), bf16),
                pltpu.VMEM((3, SIDE, ch, SIDE * group), bf16),
                pltpu.VMEM((SIDE, SIDE, SIDE, ch, width), bf16),
                pltpu.VMEM((3, group, length), f32),
                pltpu.VMEM((2, 8, group), f32),
                pltpu.VMEM((2, 8, group), f32),
                pltpu.VMEM((length, SIDE * group), bf16),
                pltpu.VMEM((SIDE, length, width), bf16),
                pltpu.VMEM((SIDE, rows, width), f32),
                pltpu.VMEM((SIDE, GENES_DEV, width), f32),
                pltpu.VMEM((SIDE, 8, width), f32),
                pltpu.VMEM((GENES_DEV, BLK), f32),
                pltpu.VMEM((8, BLK), f32),
                pltpu.VMEM((8, BLK), f32),
                pltpu.VMEM((8, length), jnp.int32),
                pltpu.SemaphoreType.DMA((160,)),
                pltpu.SemaphoreType.DMA((160,)),
                pltpu.SemaphoreType.DMA((24,)),
            ],
            compiler_params=pltpu.CompilerParams(
                collective_id=0, has_side_effects=True, vmem_limit_bytes=48 * 2**20
            ),
        )(*(pltpu.with_memory_space_constraint(operand, pltpu.HBM) for operand in operands))
        return tracks, gene_mean

    in_specs = (
        P(None, "pos", "trk"),
        P("trk"),
        P("trk"),
        P(None, None, "trk"),
        P(None, "trk"),
        P("trk"),
        P(None, "pos"),
        P("pos"),
    )
    out_specs = (P(None, "pos", "trk"), P("pos", "trk"))
    return jax.shard_map(per_device, mesh=mesh, in_specs=in_specs, out_specs=out_specs, check_vma=False)
```

time: 78.8 us -> 66.3 us (0.84)
  Pallas kernels: 72.3 us -> 64 us
  local copies, waits for them, and re-layouts: 5.57 us -> 1.59 us
    pallas_call x1, Pallas kernels: 72.3 us -> 64 us  [per_device(): pl.pallas_call(functools.partial(kernel, n_pos), name='fused_block', out_...]
    unnamed x18 -> x2, local copies, waits for them, and re-layouts: 5.57 us -> 1.59 us
where the time goes in v2:
time: 66.3 us; the launch traced here: 66.2 us
  Pallas kernels  64 us (97%)
  local copies, waits for them, and re-layouts  1.59 us (2%)
    pallas_call x1, Pallas kernels, per_device(): pl.pallas_call(functools.partial(kernel, n_pos), name='fused_block', out_...  64 us
    unnamed x2, local copies, waits for them, and re-layouts  1.59 us

profile of v2, /device:TPU:1, one launch (start us, length us, event | category | flops | bytes accessed | tf_op | source)
XLA Modules:
  0.0 66.2 jit_solution(13208284341870055651)
XLA Ops:
  0.6 64.0 %fused_block.1 = (bf16[4,512,256]{2,1,0:T(8,128)(2,1)S(1)}, f32[32,256]{1,0:T(8,128)S(1)}) custom-call(bf16[4,96,512]{2,1,0:T(8,128)(2,1)} %bitcast.9, f32[1,96]{1,0:T(1,128)} %bitcast.11, f32[1,96]{1,0:T(1,128)} %bitcast.12, bf16[3,96,1536]{2,1,0:T(8,128)(2,1)} %bitcast.7, bf16[4,4,96,256]{3,2,1,0:T(8,128)(2,1)} %bitcast.8, f32[1,256]{1,0:T(1,128)} %bitcast.10, ...), custom_call_target="tpu_custom_call" | custom-call | tf_op jit(solution)/shard_map/fused_block/pallas_call | solution.py:405
  64.6 1.0 %copy.12 = bf16[4,512,256]{2,1,0:T(8,128)(2,1)} copy(bf16[4,512,256]{2,1,0:T(8,128)(2,1)S(1)} %get-tuple-element.2) | data formatting | bytes 2097152
  65.6 0.6 copy.13

commit v3 on v2

--- a/solution.py
+++ b/solution.py
@@ -17,7 +17,7 @@
 def kernel(
     n_pos, act, gain, bias, cw, hw, hb, gs, sm,
     tracks, gene_mean,
-    gain_v, bias_v, hb_v, gs_v, sm_v, raw, small, hid, cwb, hwb, prod, edge_out, edge_in, mix, out, acc, sums_in, strad_in, cnt_own, cnt_out, cnt_in, slots,
+    gain_v, bias_v, hb_v, gs_v, sm_v, raw, small, hid, cwb, hwb, prod, edge_out, edge_in, mix, out, acc, sums_out, sums_in, strad_in, cnt_own, cnt_out, cnt_in, slots,
     send, recv, local,
 ):
     _, ch, length = act.shape
@@ -65,7 +65,7 @@
     def finish():
         for w in pending:
             w()
-        for copy in started:
+        for copy in started[-19:]:
             copy.wait_send()
 
     def remote(src, dst, device, landing):
@@ -88,35 +88,36 @@
         copy.start()
         return once(copy.wait)
 
-    partners = [dev(dy=d) for d in (1, 2, 3)] + [dev(dx=d) for d in (1, 2, 3)] + [dev(dp=d) for d in (1, -1, 2, -2)]
+    wait_vectors = [near(*pair) for pair in ((gain, gain_v), (bias, bias_v), (hb, hb_v), (gs, gs_v), (sm, sm_v))]
+
+    partners = [dev(dy=d) for d in (1, 2, 3)] + [dev(dx=d) for d in (1, 3)] + [dev(dp=d) for d in (1, -1, 2, -2)]
     partners += [dev(dp=s, dy=d) for s in (1, -1) for d in (1, 2, 3)]
     barrier = pltpu.get_barrier_semaphore()
     for partner in partners:
         pl.semaphore_signal(barrier, inc=1, device_id=partner, device_id_type=MESH)
 
-    wait_own = [near(act.at[y, :, pl.ds(c * half, half)], raw.at[y, :, pl.ds(c * half, half)]) for c in range(2)]
-    wait_vectors = [near(*pair) for pair in ((gain, gain_v), (bias, bias_v), (hb, hb_v), (gs, gs_v), (sm, sm_v))]
-    wait_cw = near(cw, cwb.at[:, y])
-    wait_hw = [near(hw.at[:, k], hwb.at[y, k]) for k in range(SIDE)]
+    pl.semaphore_wait(barrier, len(partners))
+
+    def raw_to_column(c, which):
+        cols = pl.ds(c * half, half)
+        return [
+            remote(act.at[at_y(d), :, cols], raw.at[y, :, cols], dev(dy=d), raw.at[at_y(-d), :, cols]) for d in which
+        ]
+
+    wait_raw = [raw_to_column(0, (2,))]
     small[y, :, :] = jnp.zeros(small.shape[1:], jnp.float32)
     for w in wait_vectors:
         w()
     small[y, 0:1, 0:ch] = gain_v[...]
     small[y, 1:2, 0:ch] = bias_v[...]
     small[y, 2:3, 0:width] = hb_v[...]
-    pl.semaphore_wait(barrier, len(partners))
-
-    wait_small = [remote(small.at[y], small.at[y], dev(dy=d), small.at[at_y(-d)]) for d in (1, 2, 3)]
-
-    def raw_to_column(c):
-        cols = pl.ds(c * half, half)
-        return [
-            remote(act.at[at_y(d), :, cols], raw.at[y, :, cols], dev(dy=d), raw.at[at_y(-d), :, cols]) for d in (1, 2, 3)
-        ]
-
-    def ring_first(view, spots, up, down):
-        mine = view(spots[0], None)
-        return remote(mine, mine, up, view(spots[1], None)), remote(mine, mine, down, view(spots[2], None))
+    wait_small = [remote(small.at[y], small.at[y], dev(dy=d), small.at[at_y(-d)]) for d in (2, 1, 3)]
+    wait_raw[0] += raw_to_column(0, (1, 3))
+
+    def ring_first(view, spots, up, down, mine=None):
+        here = view(spots[0], None)
+        mine = here if mine is None else mine
+        return remote(mine, here, up, view(spots[1], None)), remote(mine, here, down, view(spots[2], None))
 
     def ring_second(view, spots, up, down, waits):
         waits[0]()
@@ -208,12 +209,16 @@
 
     taps = range(3)
     cw_of = [cw_view(tap) for tap in taps]
-    wait_raw = [raw_to_column(0)]
-    wait_cw()
-    cw_ring = [ring_first(cw_of[0](q), spots_y, up_y, down_y)]
-    wait_raw.append(raw_to_column(1))
-    for tap in (1, 2):
-        cw_ring.append(ring_first(cw_of[tap](q), spots_y, up_y, down_y))
+
+    def cw_first(tap):
+        return ring_first(cw_of[tap](q), spots_y, up_y, down_y, cw.at[tap, :, lanes(q)])
+
+    cw_ring = [cw_first(0)]
+    wait_raw.append(raw_to_column(1, (2, 1, 3)))
+    wait_own = [near(act.at[y, :, pl.ds(c * half, half)], raw.at[y, :, pl.ds(c * half, half)]) for c in range(2)]
+    cw_ring += [cw_first(1), cw_first(2)]
+    wait_cw = near(cw, cwb.at[:, y])
+    wait_hw = [near(hw.at[:, k], hwb.at[y, k]) for k in range(SIDE)]
 
     rows = acc.shape[1]
     gene_ids = lax.broadcasted_iota(jnp.int32, (rows, length), 0)
@@ -250,6 +255,7 @@
 
     def product(tap, c):
         cols = pl.ds(c * half, half)
+        wait_cw()
         for w in (*cw_parts[tap][2], *hid_far[c]):
             w()
         prod[tap, :, cols] = jnp.dot(
@@ -277,7 +283,8 @@
     lane = lax.broadcasted_iota(jnp.int32, (group, BLK), 1)
     row = lax.broadcasted_iota(jnp.int32, (BLK, group), 0)
     blocks = length // BLK
-    pieces = [(b * BLK, BLK) for b in range(1, blocks)] + [(0, BLK // 2), (BLK // 2, BLK // 2)]
+    order = list(range(1, blocks)) + [0]
+    pieces = [(b * BLK, BLK) for b in order]
 
     def mixed(b):
         here = slice(b * BLK, (b + 1) * BLK)
@@ -303,30 +310,41 @@
             total += jnp.where((row == BLK - 1) & (p < n_pos - 1), edge_in[1, 0:1, :], 0.0)
         mix[here, lanes(x)] = total.astype(jnp.bfloat16)
 
-    own, tail = pl.ds(0, GENES_DEV), pl.ds(GENES_DEV, rows - GENES_DEV)
+    tail = pl.ds(GENES_DEV, rows - GENES_DEV)
     wait_sums = []
 
-    def head(first, size, final):
+    def head(first, size, beginning, final):
         here = slice(first, first + size)
         spot = pl.ds(first, size)
         onehot = (slots[0:1, here] == lax.broadcasted_iota(jnp.int32, (rows, size), 0)).astype(jnp.bfloat16)
-        for d in (2, 1, 3, 0):
-            k = at_y(d)
-            logits = jnp.dot(
-                mix[here, :], hwb[k].reshape(SIDE * group, width), preferred_element_type=jnp.float32
+        def logits(d):
+            product = jnp.dot(
+                mix[here, :], hwb[at_y(d)].reshape(SIDE * group, width), preferred_element_type=jnp.float32
             )
-            logits += small[k, 2:3, 0:width]
-            values = (jnp.maximum(logits, 0.0) + jnp.log1p(jnp.exp(-jnp.abs(logits)))).astype(jnp.bfloat16)
+            return product + small[at_y(d), 2:3, 0:width]
+
+        turns = (1, 3, 0, 2) if beginning else (2, 1, 3, 0)
+        ahead = logits(turns[0])
+        for turn, d in enumerate(turns):
+            now = ahead
+            if turn + 1 < SIDE and not (beginning and turn + 1 == SIDE - 1):
+                ahead = logits(turns[turn + 1])
+            values = (jnp.maximum(now, 0.0) + jnp.log1p(jnp.exp(-jnp.abs(now)))).astype(jnp.bfloat16)
             out[d, here, :] = values
             acc[d] += jnp.dot(onehot, values, preferred_element_type=jnp.float32)
             if final:
                 wait_sums.append(remote(acc.at[d, tail], strad_in.at[y], dev(dp=-1, dy=d), strad_in.at[at_y(-d)]))
                 if d:
-                    wait_sums.append(remote(acc.at[d, own], sums_in.at[y], dev(dy=d), sums_in.at[at_y(-d)]))
+                    sums_out[d] = acc[d, 0:GENES_DEV].astype(jnp.bfloat16)
+                    wait_sums.append(remote(sums_out.at[d], sums_in.at[y], dev(dy=d), sums_in.at[at_y(-d)]))
             if d:
                 remote(out.at[d, spot], tracks.at[y, spot], dev(dy=d), tracks.at[at_y(-d), spot])
             else:
                 near(out.at[0, spot], tracks.at[y, spot])
+            if beginning and turn + 1 == SIDE - 1:
+                for w in hw_parts[2]:
+                    w()
+                ahead = logits(turns[turn + 1])
 
     mix_ring, mix_far = [], []
 
@@ -346,30 +364,33 @@
     mixed(2)
     mix_first(1)
     weights_third(hw_view, *hw_parts)
+    mix_second(0)
     mixed(3)
-    mix_second(0)
     mix_first(2)
     weights_fourth(hw_view, *hw_parts[1:], (0, 1))
+    mix_second(1)
     mixed(0)
-    mix_second(1)
     mix_first(3)
-    mix_first(4)
     weights_fourth(hw_view, *hw_parts[1:], (2,))
-    for w in hw_parts[2]:
-        w()
+    for i in (0, 1, 3, 4):
+        hw_parts[2][i]()
     for i, piece in enumerate(pieces):
         for w in mix_far[i]:
             w()
-        head(*piece, i == len(pieces) - 1)
-        if i + 2 < len(pieces):
+        head(*piece, i == 0, i == blocks - 1)
+        if i + 2 < blocks:
             mix_second(i + 2)
 
     wait_cnt()
+    for copy in started[:-19]:
+        copy.wait_send()
+    for w in pending[:-19]:
+        w()
     for w in wait_sums:
         w()
     totals = acc[0, 0:GENES_DEV, :]
     for d in (1, 2, 3):
-        totals += sums_in[at_y(-d)]
+        totals += sums_in[at_y(-d)].astype(jnp.float32)
     strays = strad_in[0] + strad_in[1] + strad_in[2] + strad_in[3]
     counts = cnt_own[...]
     gene = lax.broadcasted_iota(jnp.int32, (GENES_DEV, width), 0)
@@ -428,7 +449,8 @@
                 pltpu.VMEM((length, SIDE * group), bf16),
                 pltpu.VMEM((SIDE, length, width), bf16),
                 pltpu.VMEM((SIDE, rows, width), f32),
-                pltpu.VMEM((SIDE, GENES_DEV, width), f32),
+                pltpu.VMEM((SIDE, GENES_DEV, width), bf16),
+                pltpu.VMEM((SIDE, GENES_DEV, width), bf16),
                 pltpu.VMEM((SIDE, 8, width), f32),
                 pltpu.VMEM((GENES_DEV, BLK), f32),
                 pltpu.VMEM((8, BLK), f32),

time: 66.3 us -> 65.2 us (0.983)
  Pallas kernels: 64 us -> 62.8 us
    pallas_call x1, Pallas kernels: 64 us -> 62.8 us  [per_device(): pl.pallas_call(functools.partial(kernel, n_pos), name='fused_block', out_...]
where the time goes in v3:
time: 65.2 us; the launch traced here: 65 us
  Pallas kernels  62.8 us (96%)
  local copies, waits for them, and re-layouts  1.59 us (2%)
    pallas_call x1, Pallas kernels, per_device(): pl.pallas_call(functools.partial(kernel, n_pos), name='fused_block', out_...  62.8 us
    unnamed x2, local copies, waits for them, and re-layouts  1.59 us

profile of v3, /device:TPU:1, one launch (start us, length us, event | category | flops | bytes accessed | tf_op | source)
XLA Modules:
  0.0 65.0 jit_solution(17578077474203124812)
XLA Ops:
  0.6 62.8 %fused_block.1 = (bf16[4,512,256]{2,1,0:T(8,128)(2,1)S(1)}, f32[32,256]{1,0:T(8,128)S(1)}) custom-call(bf16[4,96,512]{2,1,0:T(8,128)(2,1)} %bitcast.9, f32[1,96]{1,0:T(1,128)} %bitcast.11, f32[1,96]{1,0:T(1,128)} %bitcast.12, bf16[3,96,1536]{2,1,0:T(8,128)(2,1)} %bitcast.7, bf16[4,4,96,256]{3,2,1,0:T(8,128)(2,1)} %bitcast.8, f32[1,256]{1,0:T(1,128)} %bitcast.10, ...), custom_call_target="tpu_custom_call" | custom-call | tf_op jit(solution)/shard_map/fused_block/pallas_call | solution.py:426
  63.5 1.0 %copy.12 = bf16[4,512,256]{2,1,0:T(8,128)(2,1)} copy(bf16[4,512,256]{2,1,0:T(8,128)(2,1)S(1)} %get-tuple-element.2) | data formatting | bytes 2097152
  64.4 0.6 copy.13

commit v4 on v3

--- a/solution.py
+++ b/solution.py
@@ -363,23 +363,24 @@
     product(1, 1)
     mixed(2)
     mix_first(1)
+    mixed(3)
+    mix_first(2)
     weights_third(hw_view, *hw_parts)
     mix_second(0)
-    mixed(3)
-    mix_first(2)
+    mixed(0)
+    mix_first(3)
     weights_fourth(hw_view, *hw_parts[1:], (0, 1))
     mix_second(1)
-    mixed(0)
-    mix_first(3)
     weights_fourth(hw_view, *hw_parts[1:], (2,))
     for i in (0, 1, 3, 4):
         hw_parts[2][i]()
+    mix_second(2)
     for i, piece in enumerate(pieces):
         for w in mix_far[i]:
             w()
         head(*piece, i == 0, i == blocks - 1)
-        if i + 2 < blocks:
-            mix_second(i + 2)
+        if i == 0:
+            mix_second(3)
 
     wait_cnt()
     for copy in started[:-19]:

time: 65.2 us -> 66.7 us (1.023)
  Pallas kernels: 62.8 us -> 64.3 us
    pallas_call x1, Pallas kernels: 62.8 us -> 64.3 us  [per_device(): pl.pallas_call(functools.partial(kernel, n_pos), name='fused_block', out_...]
where the time goes in v4:
time: 66.7 us; the launch traced here: 66.6 us
  Pallas kernels  64.3 us (96%)
  local copies, waits for them, and re-layouts  1.59 us (2%)
    pallas_call x1, Pallas kernels, per_device(): pl.pallas_call(functools.partial(kernel, n_pos), name='fused_block', out_...  64.3 us
    unnamed x2, local copies, waits for them, and re-layouts  1.59 us

profile of v4, /device:TPU:1, one launch (start us, length us, event | category | flops | bytes accessed | tf_op | source)
XLA Modules:
  0.0 66.6 jit_solution(1648682194916632400)
XLA Ops:
  0.6 64.3 %fused_block.1 = (bf16[4,512,256]{2,1,0:T(8,128)(2,1)S(1)}, f32[32,256]{1,0:T(8,128)S(1)}) custom-call(bf16[4,96,512]{2,1,0:T(8,128)(2,1)} %bitcast.9, f32[1,96]{1,0:T(1,128)} %bitcast.11, f32[1,96]{1,0:T(1,128)} %bitcast.12, bf16[3,96,1536]{2,1,0:T(8,128)(2,1)} %bitcast.7, bf16[4,4,96,256]{3,2,1,0:T(8,128)(2,1)} %bitcast.8, f32[1,256]{1,0:T(1,128)} %bitcast.10, ...), custom_call_target="tpu_custom_call" | custom-call | tf_op jit(solution)/shard_map/fused_block/pallas_call | solution.py:427
  65.0 1.0 %copy.12 = bf16[4,512,256]{2,1,0:T(8,128)(2,1)} copy(bf16[4,512,256]{2,1,0:T(8,128)(2,1)S(1)} %get-tuple-element.2) | data formatting | bytes 2097152
  65.9 0.6 copy.13
